TPU v7x, 128 devices: a whole 4x4x4 slice. The times are simulated.
128 devices in a mesh: pts: 16 (over z, y), feat: 8 (over x, core).
Axes of the slice: x: 4, y: 4, z: 4, core: 2. Of those that a mesh axis runs over, the one named last changes fastest.
Arguments:
- points_x: float32 [3, 131072], P(None, 'pts'), may hold values from -2 to 2
- emb_x: bfloat16 [64, 131072], P(None, 'pts'), may hold values from -0.75 to 0.75
- points_y: float32 [3, 131072], P(None, 'pts'), may hold values from -2 to 2
- emb_y: bfloat16 [64, 131072], P(None, 'pts'), may hold values from -0.75 to 0.75
- mass_x: float32 [131072], P('pts'), may hold values from 0.25 to 4
- mass_y: float32 [131072], P('pts'), may hold values from 0.25 to 4
- grad_u: float32 [131072], P('pts'), may hold values from -6 to 6
- grad_v: float32 [131072], P('pts'), may hold values from -6 to 6
- omega_coord: float32 [3, 2048], P(None, 'feat'), may hold values from -4 to 4
- omega_emb: bfloat16 [64, 2048], P(None, 'feat'), may hold values from -4 to 4
Outputs:
- grad_emb_x: float32 [64, 131072], P(None, 'pts')
- grad_emb_y: float32 [64, 131072], P(None, 'pts')
All inputs are finite; a program needn't handle non-finite values.
Results may differ from a plain program's by a relative error of at most 0.0003.
Values may be sent and summed in bfloat16 or wider, within the bound.
A program may use at most 192 MiB of HBM per device.

v0:
```python
import jax
import jax.numpy as jnp
from jax import lax
from jax.sharding import PartitionSpec as P

ITERS = 3


highest = lax.Precision.HIGHEST


def feature_map(points, embedding, coord_seed, emb_seed):
    linear = lax.dot_general(
        emb_seed, embedding, (((0,), (0,)), ((), ())), preferred_element_type=jnp.float32
    )
    linear = linear + lax.dot_general(
        coord_seed,
        points,
        (((0,), (0,)), ((), ())),
        precision=highest,
        preferred_element_type=jnp.float32,
    )
    emb_wide = embedding.astype(jnp.float32)
    half_norm = 0.5 * (jnp.sum(points * points, axis=0) + jnp.sum(emb_wide * emb_wide, axis=0))
    return jnp.exp(linear - half_norm[None, :])


def block_terms(feats, rows, cols, emb_seed):
    bar_s = (
        lax.dot_general(
            rows,
            cols,
            (((0,), (0,)), ((), ())),
            precision=highest,
            preferred_element_type=jnp.float32,
        )
        * feats
    )
    total = jnp.dot(emb_seed.astype(jnp.float32), bar_s, precision=highest)
    return (total, jnp.sum(bar_s, axis=0))


def transport_reverse_pass(
    feat_x, feat_y, mass_x, mass_y, grad_u, grad_v, scaling, over_points, over_features
):
    count = feat_x.shape[1]
    dual_v = jnp.ones((count,), jnp.float32)
    saved = []
    for step in range(ITERS):
        col_c = over_points(jnp.dot(feat_y, dual_v, precision=highest))
        kern_v = scaling * over_features(jnp.dot(col_c, feat_x, precision=highest))
        dual_u = jnp.sqrt(mass_x / kern_v)
        col_d = over_points(jnp.dot(feat_x, dual_u, precision=highest))
        kern_u = scaling * over_features(jnp.dot(col_d, feat_y, precision=highest))
        new_v = jnp.sqrt(mass_y / kern_u)
        saved.append((dual_v, col_c, kern_v, dual_u, col_d, kern_u, new_v))
        dual_v = new_v
    back_v = grad_v
    x_rows, x_cols, y_rows, y_cols = ([], [], [], [])
    for step in reversed(range(ITERS)):
        prev_v, col_c, kern_v, dual_u, col_d, kern_u, new_v = saved[step]
        back_ku = -0.5 * new_v * back_v / kern_u
        back_d = scaling * over_points(jnp.dot(feat_y, back_ku, precision=highest))
        back_u = over_features(jnp.dot(back_d, feat_x, precision=highest))
        if step == ITERS - 1:
            back_u = back_u + grad_u
        reverse_kernel_value = -0.5 * dual_u * back_u / kern_v
        back_c = scaling * over_points(jnp.dot(feat_x, reverse_kernel_value, precision=highest))
        if step > 0:
            back_v = over_features(jnp.dot(back_c, feat_y, precision=highest))
        x_rows += [back_d, scaling * col_c]
        x_cols += [dual_u, reverse_kernel_value]
        y_rows += [scaling * col_d, back_c]
        y_cols += [back_ku, prev_v]
    return (jnp.stack(x_rows), jnp.stack(x_cols), jnp.stack(y_rows), jnp.stack(y_cols))


def per_device(
    points_x, emb_x, points_y, emb_y, mass_x, mass_y, grad_u, grad_v, omega_coord, omega_emb
):
    count = points_x.shape[1]
    total_points = count * lax.axis_size("pts")
    feat_x = feature_map(points_x, emb_x, omega_coord, omega_emb)
    feat_y = feature_map(points_y, emb_y, omega_coord, omega_emb)
    scaling = 1.0 / (feat_x.shape[0] * lax.axis_size("feat") * total_points)

    def over_points(vector):
        return lax.psum(vector, "pts")

    def over_features(vector):
        return lax.psum(vector, "feat")

    source_rows, source_columns, target_rows, target_columns = transport_reverse_pass(
        feat_x, feat_y, mass_x, mass_y, grad_u, grad_v, scaling, over_points, over_features
    )
    wide_x = emb_x.astype(jnp.float32)
    wide_y = emb_y.astype(jnp.float32)
    total_x, sums_x = block_terms(feat_x, source_rows, source_columns, omega_emb)
    total_y, sums_y = block_terms(feat_y, target_rows, target_columns, omega_emb)
    share_x = total_x - wide_x * sums_x[None, :]
    share_y = total_y - wide_y * sums_y[None, :]
    grad_x, grad_y = lax.psum((share_x, share_y), "feat")
    return (grad_x, grad_y)


def solution(mesh):
    in_specs = (
        P(None, "pts"),
        P(None, "pts"),
        P(None, "pts"),
        P(None, "pts"),
        P("pts"),
        P("pts"),
        P("pts"),
        P("pts"),
        P(None, "feat"),
        P(None, "feat"),
    )
    out_specs = (P(None, "pts"), P(None, "pts"))
    return jax.shard_map(
        per_device, mesh=mesh, in_specs=in_specs, out_specs=out_specs, check_vma=False
    )
```

profile of v0, /device:TPU:0, one launch (start us, length us, event | category | flops | bytes accessed | tf_op | source)
XLA Modules:
  0.0 1038.0 jit_solution(514237571591043715)
XLA Ops:
  33.7 42.0 %psum.175 = f32[256]{0:T(256)S(1)} all-reduce(f32[256]{0:T(256)S(1)} %bitcast.186), channel_id=1, replica_groups=mesh['pts'=16,'feat'=8] {'pts'}, use_global_device_ids=true, to_apply=%region_4.0 | all-reduce | flops 256 | bytes 2048 | tf_op jit(solution)/shard_map/psum | solution.py:88
  92.9 23.8 %psum.176 = f32[8192]{0:T(1024)S(1)} all-reduce(f32[8192]{0:T(1024)S(1)} %bitcast.159), channel_id=1, replica_groups=mesh['pts'=16,'feat'=8] {'feat'}, use_global_device_ids=true, to_apply=%region_5.0 | all-reduce | flops 8192 | bytes 65536 | tf_op jit(solution)/shard_map/psum | solution.py:91
  125.7 35.5 %psum.177 = f32[256]{0:T(256)S(1)} all-reduce(f32[256]{0:T(256)S(1)} %bitcast.187), channel_id=1, replica_groups=mesh['pts'=16,'feat'=8] {'pts'}, use_global_device_ids=true, to_apply=%region_6.0 | all-reduce | flops 256 | bytes 2048 | tf_op jit(solution)/shard_map/psum | solution.py:88
  168.5 23.6 %psum.178 = f32[8192]{0:T(1024)S(1)} all-reduce(f32[8192]{0:T(1024)S(1)} %bitcast.160), channel_id=1, replica_groups=mesh['pts'=16,'feat'=8] {'feat'}, use_global_device_ids=true, to_apply=%region_7.0 | all-reduce | flops 8192 | bytes 65536 | tf_op jit(solution)/shard_map/psum | solution.py:91
  201.0 37.9 %psum.179 = f32[256]{0:T(256)S(1)} all-reduce(f32[256]{0:T(256)S(1)} %bitcast.188), channel_id=1, replica_groups=mesh['pts'=16,'feat'=8] {'pts'}, use_global_device_ids=true, to_apply=%region_8.0 | all-reduce | flops 256 | bytes 2048 | tf_op jit(solution)/shard_map/psum | solution.py:88
  246.3 23.6 %psum.180 = f32[8192]{0:T(1024)S(1)} all-reduce(f32[8192]{0:T(1024)S(1)} %bitcast.161), channel_id=1, replica_groups=mesh['pts'=16,'feat'=8] {'feat'}, use_global_device_ids=true, to_apply=%region_9.0 | all-reduce | flops 8192 | bytes 65536 | tf_op jit(solution)/shard_map/psum | solution.py:91
  278.8 35.5 %psum.181 = f32[256]{0:T(256)S(1)} all-reduce(f32[256]{0:T(256)S(1)} %bitcast.189), channel_id=1, replica_groups=mesh['pts'=16,'feat'=8] {'pts'}, use_global_device_ids=true, to_apply=%region_10.0 | all-reduce | flops 256 | bytes 2048 | tf_op jit(solution)/shard_map/psum | solution.py:88
  321.7 23.8 %psum.182 = f32[8192]{0:T(1024)S(1)} all-reduce(f32[8192]{0:T(1024)S(1)} %bitcast.162), channel_id=1, replica_groups=mesh['pts'=16,'feat'=8] {'feat'}, use_global_device_ids=true, to_apply=%region_11.0 | all-reduce | flops 8192 | bytes 65536 | tf_op jit(solution)/shard_map/psum | solution.py:91
  354.4 37.5 %psum.183 = f32[256]{0:T(256)S(1)} all-reduce(f32[256]{0:T(256)S(1)} %bitcast.190), channel_id=1, replica_groups=mesh['pts'=16,'feat'=8] {'pts'}, use_global_device_ids=true, to_apply=%region_12.0 | all-reduce | flops 256 | bytes 2048 | tf_op jit(solution)/shard_map/psum | solution.py:88
  399.3 23.6 %psum.184 = f32[8192]{0:T(1024)S(1)} all-reduce(f32[8192]{0:T(1024)S(1)} %bitcast.163), channel_id=1, replica_groups=mesh['pts'=16,'feat'=8] {'feat'}, use_global_device_ids=true, to_apply=%region_13.0 | all-reduce | flops 8192 | bytes 65536 | tf_op jit(solution)/shard_map/psum | solution.py:91
  431.8 35.7 %psum.185 = f32[256]{0:T(256)S(1)} all-reduce(f32[256]{0:T(256)S(1)} %bitcast.191), channel_id=1, replica_groups=mesh['pts'=16,'feat'=8] {'pts'}, use_global_device_ids=true, to_apply=%region_14.0 | all-reduce | flops 256 | bytes 2048 | tf_op jit(solution)/shard_map/psum | solution.py:88
  474.9 23.6 %psum.186 = f32[8192]{0:T(1024)S(1)} all-reduce(f32[8192]{0:T(1024)S(1)} %bitcast.164), channel_id=1, replica_groups=mesh['pts'=16,'feat'=8] {'feat'}, use_global_device_ids=true, to_apply=%region_15.0 | all-reduce | flops 8192 | bytes 65536 | tf_op jit(solution)/shard_map/psum | solution.py:91
  507.4 37.5 %psum.187 = f32[256]{0:T(256)S(1)} all-reduce(f32[256]{0:T(256)S(1)} %bitcast.192), channel_id=1, replica_groups=mesh['pts'=16,'feat'=8] {'pts'}, use_global_device_ids=true, to_apply=%region_16.0 | all-reduce | flops 256 | bytes 2048 | tf_op jit(solution)/shard_map/psum | solution.py:88
  552.3 24.0 %psum.188 = f32[8192]{0:T(1024)S(1)} all-reduce(f32[8192]{0:T(1024)S(1)} %bitcast.165), channel_id=1, replica_groups=mesh['pts'=16,'feat'=8] {'feat'}, use_global_device_ids=true, to_apply=%region_17.0 | all-reduce | flops 8192 | bytes 65536 | tf_op jit(solution)/shard_map/psum | solution.py:91
  585.2 35.5 %psum.189 = f32[256]{0:T(256)S(1)} all-reduce(f32[256]{0:T(256)S(1)} %bitcast.193), channel_id=1, replica_groups=mesh['pts'=16,'feat'=8] {'pts'}, use_global_device_ids=true, to_apply=%region_18.0 | all-reduce | flops 256 | bytes 2048 | tf_op jit(solution)/shard_map/psum | solution.py:88
  628.1 23.6 %psum.190 = f32[8192]{0:T(1024)S(1)} all-reduce(f32[8192]{0:T(1024)S(1)} %bitcast.166), channel_id=1, replica_groups=mesh['pts'=16,'feat'=8] {'feat'}, use_global_device_ids=true, to_apply=%region_19.0 | all-reduce | flops 8192 | bytes 65536 | tf_op jit(solution)/shard_map/psum | solution.py:91
  660.6 37.6 %psum.191 = f32[256]{0:T(256)S(1)} all-reduce(f32[256]{0:T(256)S(1)} %bitcast.194), channel_id=1, replica_groups=mesh['pts'=16,'feat'=8] {'pts'}, use_global_device_ids=true, to_apply=%region_20.0 | all-reduce | flops 256 | bytes 2048 | tf_op jit(solution)/shard_map/psum | solution.py:88
  705.7 23.6 %psum.192 = f32[8192]{0:T(1024)S(1)} all-reduce(f32[8192]{0:T(1024)S(1)} %bitcast.167), channel_id=1, replica_groups=mesh['pts'=16,'feat'=8] {'feat'}, use_global_device_ids=true, to_apply=%region_21.0 | all-reduce | flops 8192 | bytes 65536 | tf_op jit(solution)/shard_map/psum | solution.py:91
  738.2 35.5 %psum.193 = f32[256]{0:T(256)S(1)} all-reduce(f32[256]{0:T(256)S(1)} %bitcast.195), channel_id=1, replica_groups=mesh['pts'=16,'feat'=8] {'pts'}, use_global_device_ids=true, to_apply=%region_22.0 | all-reduce | flops 256 | bytes 2048 | tf_op jit(solution)/shard_map/psum | solution.py:88
  781.0 23.8 %psum.194 = f32[8192]{0:T(1024)S(1)} all-reduce(f32[8192]{0:T(1024)S(1)} %bitcast.168), channel_id=1, replica_groups=mesh['pts'=16,'feat'=8] {'feat'}, use_global_device_ids=true, to_apply=%region_23.0 | all-reduce | flops 8192 | bytes 65536 | tf_op jit(solution)/shard_map/psum | solution.py:91
  813.8 37.5 %psum.195 = f32[256]{0:T(256)S(1)} all-reduce(f32[256]{0:T(256)S(1)} %bitcast.196), channel_id=1, replica_groups=mesh['pts'=16,'feat'=8] {'pts'}, use_global_device_ids=true, to_apply=%region_24.0 | all-reduce | flops 256 | bytes 2048 | tf_op jit(solution)/shard_map/psum | solution.py:88
  858.7 23.6 %psum.196 = f32[8192]{0:T(1024)S(1)} all-reduce(f32[8192]{0:T(1024)S(1)} %bitcast.169), channel_id=1, replica_groups=mesh['pts'=16,'feat'=8] {'feat'}, use_global_device_ids=true, to_apply=%region_25.0 | all-reduce | flops 8192 | bytes 65536 | tf_op jit(solution)/shard_map/psum | solution.py:91
  891.2 35.9 %psum.198 = f32[256]{0:T(256)S(1)} all-reduce(f32[256]{0:T(256)S(1)} %bitcast.197), channel_id=1, replica_groups=mesh['pts'=16,'feat'=8] {'pts'}, use_global_device_ids=true, to_apply=%region_28.0 | all-reduce | flops 256 | bytes 2048 | tf_op jit(solution)/shard_map/psum | solution.py:88
  956.9 68.0 %all-reduce.3.cloned.1.call-done = (f32[64,8192]{1,0:T(8,128)}, f32[64,8192]{1,0:T(8,128)}) async-done(((f32[64,8192]{1,0:T(8,128)}, f32[64,8192]{1,0:T(8,128)}), (f32[64,8192]{1,0:T(8,128)}, f32[64,8192]{1,0:T(8,128)})) %all-reduce.3.cloned.1.call-update) | async-done | bytes 4194320 | tf_op jit(solution)/shard_map/psum | solution.py:102
  (93 shorter events, 251.8 us)
Async XLA Ops:
  7.2 1.6 copy-start
  7.2 4.2 copy-start.4
  7.2 1017.7 %all-reduce.3.cloned.1.call-start = ((), (), s32[]{:S(2)}) async-start(), calls=%async_computation | async-start | bytes 8388608 | tf_op jit(solution)/shard_map/psum | solution.py:102
  8.8 7.3 copy-start.7
  8.8 7.4 copy-start.11
  23.7 3.2 copy-start.2
  27.0 48.8 %copy-start.8 = (f32[3,8192]{1,0:T(4,128)S(1)}, f32[3,8192]{1,0:T(4,128)}, u32[]{:S(2)}) copy-start(f32[3,8192]{1,0:T(4,128)} %param.10) | copy-start | bytes 294916
  85.7 3.2 copy-start.1
  85.7 31.0 %copy-start.5 = (f32[8192]{0:T(1024)S(1)}, f32[8192]{0:T(1024)}, u32[]{:S(2)}) copy-start(f32[8192]{0:T(1024)} %param.14) | copy-start | bytes 98308
  116.8 75.4 %copy-start.6 = (f32[8192]{0:T(1024)S(1)}, f32[8192]{0:T(1024)}, u32[]{:S(2)}) copy-start(f32[8192]{0:T(1024)} %param.15) | copy-start | bytes 98308
  422.9 75.6 %copy-start.10 = (f32[8192]{0:T(1024)S(1)}, f32[8192]{0:T(1024)}, u32[]{:S(2)}) copy-start(f32[8192]{0:T(1024)} %param.17) | copy-start | bytes 98308
  498.5 77.8 %copy-start.9 = (f32[8192]{0:T(1024)S(1)}, f32[8192]{0:T(1024)}, u32[]{:S(2)}) copy-start(f32[8192]{0:T(1024)} %param.16) | copy-start | bytes 98308
  927.4 9.6 copy-start.3
Sparse Core Ops, SparseCore 0:
  957.0 67.7 all-reduce.2
where the time goes:
time: 1050 us; the launch traced here: 1040 us
  blocking collectives  704 us (67%)
  matrix products  236 us (22%)
  waiting for transfers between devices  68 us (6%)
  between operations  14.5 us (1%)
  local copies, waits for them, and re-layouts  13.2 us (1%)
    psum x12, blocking collectives, over_points(): return lax.psum(vector, 'pts')  443 us
    psum x11, blocking collectives, over_features(): return lax.psum(vector, 'feat')  260 us
    psum x1, waiting for transfers between devices, per_device(): grad_x, grad_y = lax.psum((share_x, share_y), 'feat')  68 us
    dot_general x3, matrix products, transport_reverse_pass(): col_d = over_points(jnp.dot(feat_x, dual_u, precision=highest))  26.7 us
    dot_general x3, matrix products, transport_reverse_pass(): back_d = scaling * over_points(jnp.dot(feat_y, back_ku, precision=highest))  26.7 us
    dot_general x3, matrix products, transport_reverse_pass(): jnp.dot(feat_x, reverse_kernel_value, precision=highest)  26.7 us
    dot_general x3, matrix products, transport_reverse_pass(): col_c = over_points(jnp.dot(feat_y, dual_v, precision=highest))  24.5 us
    dot_general x3, matrix products, transport_reverse_pass(): back_u = over_features(jnp.dot(back_d, feat_x, precision=highest))  22.2 us
  transfers between devices with their start and end apart: 1, of which 1 were waited for; matrix products, arithmetic and copies ran while one was open for 0% of the time, Pallas kernels for 0%

commit v1 on v0

v1 whole, which is shorter than its diff:
```python
import jax
import jax.numpy as jnp
from jax import lax
from jax.experimental import pallas as pl
from jax.experimental.pallas import tpu as pltpu
from jax.sharding import PartitionSpec as P

MESH = pl.DeviceIdType.MESH
F32, BF16 = jnp.float32, jnp.bfloat16
SCALING = 1.0 / 268435456
STEPS = 3
PTS = 2048
FEATS = 1024
ROUNDS = 4 * STEPS
HALF = PTS // 2


def hop(k):
    return min(k, 4 - k)


OFFSETS = sorted(
    ((a, b, d) for a in range(4) for b in range(4) for d in range(4) if a or b or d),
    key=lambda o: -(hop(o[0]) + hop(o[1]) + hop(o[2])),
)
PEERS = len(OFFSETS)


def split3(v):
    one = v.astype(BF16).astype(F32)
    rest = v - one
    two = rest.astype(BF16).astype(F32)
    return one, two, (rest - two).astype(BF16).astype(F32)


def split2(v):
    one = v.astype(BF16)
    return one, (v - one.astype(F32)).astype(BF16)


def tree(terms):
    terms = list(terms)
    while len(terms) > 1:
        terms = [
            terms[i] + terms[i + 1] if i + 1 < len(terms) else terms[i]
            for i in range(0, len(terms), 2)
        ]
    return terms[0]


def kernel(
    points_x, emb_x, points_y, emb_y, mass_x, mass_y, grad_u, grad_v, coord, seeds,
    out_x, out_y,
    feat_x, feat_y, pts_in, emb_in, vec_in, om_c, om_e, om_ext, om_stage, om_t, xs_stage, xs_x, xs_y,
    acc, cb, send, buf, ksend, krecv, rows_c, rows_d, rows_bd, rows_bc,
    col_u, col_v, col_kv, col_ku, col_bku, col_bkv, terms_a, terms_b, total_x, total_y,
    gsend, grecv, own,
    in_sem, om_send, om_recv, send_sem, recv_sem, k_send, k_recv, g_send, g_recv,
    o_local, o_send, o_recv, f_send, f_recv,
):
    p, f = lax.axis_index("pts"), lax.axis_index("feat")
    z, y, x, c = p // 4, p % 4, f // 2, f % 2
    sibling = (p, x * 2 + (1 - c))
    planes = [[((z + a) % 4) * 4 + (y + b) % 4 for b in range(4)] for a in range(4)]
    along = [((x + d) % 4) * 2 + c for d in range(4)]
    chips = [(planes[a][b], along[d]) for a, b, d in OFFSETS]
    ring = [(p, along[d]) for d in (2, 1, 3)]

    barrier = pltpu.get_barrier_semaphore()
    for device in chips + [sibling]:
        pl.semaphore_signal(barrier, inc=1, device_id=device, device_id_type=MESH)

    lanes = pl.ds(pl.multiple_of(x * PTS, PTS), PTS)
    rows16 = pl.ds(pl.multiple_of(x * 16, 16), 16)
    loads = [
        pltpu.make_async_copy(points_x.at[:, lanes], pts_in.at[0], in_sem.at[0]),
        pltpu.make_async_copy(points_y.at[:, lanes], pts_in.at[1], in_sem.at[1]),
        pltpu.make_async_copy(emb_x.at[:, lanes], emb_in.at[0], in_sem.at[2]),
        pltpu.make_async_copy(emb_y.at[:, lanes], emb_in.at[1], in_sem.at[3]),
    ] + [
        pltpu.make_async_copy(ref.at[rows16, :], vec_in.at[i], in_sem.at[4 + i])
        for i, ref in enumerate((mass_x, mass_y, grad_u, grad_v))
    ]
    for load in loads:
        load.start()

    total_x[...] = jnp.zeros_like(total_x)
    total_y[...] = jnp.zeros_like(total_y)
    om_stage[...] = jnp.zeros_like(om_stage)
    xs_stage[...] = jnp.zeros_like(xs_stage)
    terms_a[...] = jnp.zeros_like(terms_a)
    terms_b[...] = jnp.zeros_like(terms_b)
    om_ext[...] = jnp.zeros_like(om_ext)
    rows_bc[STEPS + 1] = jnp.zeros((8, 128), F32)
    col_v[0] = jnp.ones((16, 128), F32)
    for load in loads:
        load.wait()

    for which, ref in ((0, xs_x), (1, xs_y)):
        pts = pts_in[which]
        wide = emb_in[which].astype(F32)
        half = 0.5 * (
            jnp.sum(pts * pts, axis=0, keepdims=True)
            + jnp.sum(wide * wide, axis=0, keepdims=True)
        )
        p1, p2, p3 = split3(pts)
        for i, part in enumerate((p1, p2, p3, p1, p2, p1)):
            xs_stage[3 * i : 3 * i + 3, :] = part
        for i, part in enumerate(split3(-half)):
            xs_stage[18 + i : 19 + i, :] = part
        ref[0:64, :] = emb_in[which]
        ref[64:128, :] = xs_stage[...].astype(BF16)

    pl.semaphore_wait(barrier, PEERS + 1)
    om_e[x] = seeds[...]
    om_c[x] = coord[...]
    om_copies = []
    for i, device in enumerate(ring):
        for k, ref in enumerate((om_e, om_c)):
            copy = pltpu.make_async_remote_copy(
                src_ref=ref.at[x], dst_ref=ref.at[x], send_sem=om_send.at[k, i],
                recv_sem=om_recv.at[k], device_id=device, device_id_type=MESH,
            )
            copy.start()
            om_copies.append(copy)
    for k, ref in enumerate((om_e, om_c)):
        three = ref.at[pl.ds(0, 3)]
        pltpu.make_async_copy(three, three, om_recv.at[k]).wait()
    for copy in om_copies:
        copy.wait_send()
    for s in range(4):
        om_stage[0:64, :] = om_e[s].astype(F32)
        o1, o2, o3 = split3(om_c[s])
        for i, part in enumerate((o1, o1, o1, o2, o2, o3)):
            om_stage[64 + 3 * i : 67 + 3 * i, :] = part
        om_stage[82:85, :] = jnp.ones((3, 256), F32)
        om_t[s * 256 : (s + 1) * 256, :] = om_stage[...].T.astype(BF16)
        om_ext[0:64, s * 256 : (s + 1) * 256] = om_e[s]
    om_ext[64:80, :] = jnp.where(
        lax.broadcasted_iota(jnp.int32, (16, FEATS), 0) == 0, 1.0, 0.0
    ).astype(BF16)

    def build(feat, xs):
        def block(i, _):
            r = pl.ds(pl.multiple_of((i // 4) * 256, 256), 256)
            l = pl.ds(pl.multiple_of((i % 4) * 512, 512), 512)
            feat[r, l] = jnp.exp(jnp.dot(om_t[r, :], xs[:, l], preferred_element_type=F32))
            return 0

        lax.fori_loop(0, 16, block, 0)

    row_at = lax.broadcasted_iota(jnp.int32, (8, 128), 0)

    def round_start(r):
        ones = jnp.ones((8, 128), BF16)
        parts = [
            lax.dot_general(
                ones, part.astype(BF16), (((1,), (1,)), ((), ())), preferred_element_type=F32
            )
            for part in split3(acc[...])
        ]
        flat = parts[0] + (parts[1] + parts[2])
        own_sum = flat[:, 0:128]
        for a in range(1, 8):
            own_sum = jnp.where(row_at == a, flat[:, a * 128 : (a + 1) * 128], own_sum)
        send[r] = own_sum
        for k, device in enumerate(chips):
            pltpu.make_async_remote_copy(
                src_ref=send.at[r], dst_ref=buf.at[r, k], send_sem=send_sem.at[r],
                recv_sem=recv_sem.at[r], device_id=device, device_id_type=MESH,
            ).start()

    def round_wait(r):
        pltpu.make_async_copy(buf.at[r], buf.at[r], recv_sem.at[r]).wait()
        return tree([send[r]] + [buf[r, k] for k in range(PEERS)])

    def spread(value):
        turned = value.T
        for a in range(8):
            cb[a * 128 : (a + 1) * 128, :] = jnp.broadcast_to(turned[:, a : a + 1], (128, 128))

    def over_features(feat, r):
        for h in range(2):

            def block(i, sums):
                sums = list(sums)
                for k in range(8):
                    rows = pl.ds(pl.multiple_of(i * 64, 64) + 8 * k, 8)
                    weight = cb[rows, :]
                    for j in range(8):
                        at = h * HALF + j * 128
                        sums[j] = sums[j] + feat[rows, at : at + 128] * weight
                return tuple(sums)

            sums = lax.fori_loop(
                0, FEATS // 64, block, tuple(jnp.zeros((8, 128), F32) for _ in range(8))
            )
            for j in range(8):
                ksend[r, h, j : j + 1, :] = jnp.sum(sums[j], axis=0, keepdims=True)
            pltpu.make_async_remote_copy(
                src_ref=ksend.at[r, h], dst_ref=krecv.at[r, h], send_sem=k_send.at[r, h],
                recv_sem=k_recv.at[r, h], device_id=sibling, device_id_type=MESH,
            ).start()

    def over_points(feat, h, weights):
        spreads = [jnp.broadcast_to(weights[j : j + 1, :], (8, 128)) for j in range(8)]

        def block(i, _):
            for k in range(8):
                rows = pl.ds(pl.multiple_of(i * 64, 64) + 8 * k, 8)
                part = tree(
                    feat[rows, h * HALF + j * 128 : h * HALF + (j + 1) * 128] * spreads[j]
                    for j in range(8)
                )
                acc[rows, :] = part if h == 0 else acc[rows, :] + part
            return 0

        lax.fori_loop(0, FEATS // 64, block, 0)

    def half_step(feat, r, update):
        over_features(feat, r)
        for h in range(2):
            pltpu.make_async_copy(krecv.at[r, h], krecv.at[r, h], k_recv.at[r, h]).wait()
            over_points(feat, h, update(pl.ds(h * 8, 8), ksend[r, h] + krecv[r, h]))

    def add_terms(feat, total, pairs):
        for i, (row, col) in enumerate(pairs):
            r1, r2 = (v.astype(F32) for v in split2(row))
            c1, c2 = (v.astype(F32) for v in split2(col))
            for k, (left, right) in enumerate(((r1, c1), (r1, c2), (r2, c1))):
                at = 3 * i + k
                for a in range(8):
                    terms_a[at : at + 1, a * 128 : (a + 1) * 128] = left[a : a + 1, :]
                for a in range(16):
                    terms_b[at : at + 1, a * 128 : (a + 1) * 128] = right[a : a + 1, :]

        def block(i, _):
            r = pl.ds(pl.multiple_of((i % 4) * 256, 256), 256)
            l = pl.ds(pl.multiple_of((i // 4) * 512, 512), 512)
            weight = lax.dot_general(
                terms_a[:, r].astype(BF16), terms_b[:, l].astype(BF16),
                (((0,), (0,)), ((), ())), preferred_element_type=F32,
            )
            hi, lo = split2(feat[r, l] * weight)
            left = om_ext[:, r]
            total[:, l] += jnp.dot(left, hi, preferred_element_type=F32) + jnp.dot(
                left, lo, preferred_element_type=F32
            )
            return 0

        lax.fori_loop(0, 16, block, 0)

    def finish(which, total):
        wide = emb_in[which].astype(F32)
        share = total[0:64, :] - wide * total[64:65, :]
        first, second = share[:, :HALF], share[:, HALF:]
        own[which] = jnp.where(c == 0, first, second)
        gsend[which] = jnp.where(c == 0, second, first)
        pltpu.make_async_remote_copy(
            src_ref=gsend.at[which], dst_ref=grecv.at[which], send_sem=g_send.at[which],
            recv_sem=g_recv.at[which], device_id=sibling, device_id_type=MESH,
        ).start()

    def place(which, out):
        pltpu.make_async_copy(grecv.at[which], grecv.at[which], g_recv.at[which]).wait()
        own[which] = own[which] + grecv[which]
        mine = out.at[:, pl.ds(pl.multiple_of(x * PTS + c * HALF, HALF), HALF)]
        for k, device in enumerate(ring + [sibling]):
            pltpu.make_async_remote_copy(
                src_ref=own.at[which], dst_ref=mine, send_sem=o_send.at[which, k],
                recv_sem=o_recv.at[which, k], device_id=device, device_id_type=MESH,
            ).start()
        pltpu.make_async_copy(own.at[which], mine, o_local.at[which]).start()

    def theirs(out, d, core):
        return out.at[:, pl.ds(pl.multiple_of(((x + 4 - d) % 4) * PTS + core * HALF, HALF), HALF)]

    build(feat_y, xs_y)
    for h in range(2):
        over_points(feat_y, h, jnp.ones((8, 128), F32))
    round_start(0)
    build(feat_x, xs_x)

    def forward(i, _):
        t = i + 1
        value = round_wait(2 * i)
        rows_c[t] = SCALING * value
        spread(value)

        def update_u(at, sums):
            kern = SCALING * sums
            dual = jnp.sqrt(vec_in[0, at, :] / kern)
            col_kv[t, at, :] = kern
            col_u[t, at, :] = dual
            return dual

        half_step(feat_x, 2 * i, update_u)
        round_start(2 * i + 1)
        value = round_wait(2 * i + 1)
        rows_d[t] = SCALING * value
        spread(value)

        def update_v(at, sums):
            kern = SCALING * sums
            dual = jnp.sqrt(vec_in[1, at, :] / kern)
            back = -0.5 * dual * vec_in[3, at, :] / kern
            col_ku[t, at, :] = kern
            col_v[t, at, :] = dual
            col_bku[t, at, :] = back
            return jnp.where(t == STEPS, back, dual)

        half_step(feat_y, 2 * i + 1, update_v)
        round_start(2 * i + 2)
        return 0

    lax.fori_loop(0, STEPS, forward, 0)

    def backward_x(j):
        t = STEPS - j
        r = 2 * STEPS + 2 * j
        add_terms(feat_y, total_y, ((rows_d[t], col_bku[t]), (rows_bc[t + 1], col_v[t])))
        value = SCALING * round_wait(r)
        rows_bd[t] = value
        spread(value)

        def update(at, sums):
            back_u = sums + jnp.where(t == STEPS, vec_in[2, at, :], 0.0)
            back = -0.5 * col_u[t, at, :] * back_u / col_kv[t, at, :]
            col_bkv[t, at, :] = back
            return back

        half_step(feat_x, r, update)
        round_start(r + 1)
        add_terms(feat_x, total_x, ((rows_bd[t], col_u[t]), (rows_c[t], col_bkv[t])))

    def backward(j, _):
        t = STEPS - j
        r = 2 * STEPS + 2 * j + 1
        backward_x(j)
        value = SCALING * round_wait(r)
        rows_bc[t] = value
        spread(value)

        def update(at, sums):
            back = -0.5 * col_v[t - 1, at, :] * sums / col_ku[t - 1, at, :]
            col_bku[t - 1, at, :] = back
            return back

        half_step(feat_y, r, update)
        round_start(r + 1)
        return 0

    lax.fori_loop(0, STEPS - 1, backward, 0)
    backward_x(STEPS - 1)
    finish(0, total_x)
    place(0, out_x)
    value = SCALING * round_wait(ROUNDS - 1)
    zero = jnp.zeros((16, 128), F32)
    add_terms(feat_y, total_y, ((value, col_v[0]), (jnp.zeros((8, 128), F32), zero)))
    finish(1, total_y)
    place(1, out_y)

    for which, out in ((0, out_x), (1, out_y)):
        for k, d in enumerate((2, 1, 3)):
            block = theirs(out, d, c)
            pltpu.make_async_copy(block, block, o_recv.at[which, k]).wait()
            pltpu.make_async_remote_copy(
                src_ref=block, dst_ref=block, send_sem=f_send.at[which, k],
                recv_sem=f_recv.at[which, k], device_id=sibling, device_id_type=MESH,
            ).start()
    for which, out in ((0, out_x), (1, out_y)):
        pltpu.make_async_copy(own.at[which], theirs(out, 0, c), o_local.at[which]).wait()
        other = theirs(out, 0, 1 - c)
        pltpu.make_async_copy(other, other, o_recv.at[which, 3]).wait()
        for k, d in enumerate((2, 1, 3)):
            other = theirs(out, d, 1 - c)
            pltpu.make_async_copy(other, other, f_recv.at[which, k]).wait()
            block = theirs(out, d, c)
            pltpu.make_async_copy(block, block, f_send.at[which, k]).wait()
        for k in range(4):
            pltpu.make_async_copy(own.at[which], own.at[which], o_send.at[which, k]).wait()
        pltpu.make_async_copy(gsend.at[which], gsend.at[which], g_send.at[which]).wait()

    def drain(r, _):
        pltpu.make_async_copy(buf.at[r], buf.at[r], send_sem.at[r]).wait()
        return 0

    lax.fori_loop(0, ROUNDS, drain, 0)

    def drain_k(r, _):
        for h in range(2):
            pltpu.make_async_copy(ksend.at[r, h], ksend.at[r, h], k_send.at[r, h]).wait()
        return 0

    lax.fori_loop(0, ROUNDS - 1, drain_k, 0)


def per_device(
    points_x, emb_x, points_y, emb_y, mass_x, mass_y, grad_u, grad_v, omega_coord, omega_emb
):
    vectors = [v.reshape(64, 128) for v in (mass_x, mass_y, grad_u, grad_v)]
    hbm = pl.BlockSpec(memory_space=pl.ANY)
    vmem = pl.BlockSpec(memory_space=pltpu.VMEM)
    out = jax.ShapeDtypeStruct((64, 4 * PTS), F32)
    dma = pltpu.SemaphoreType.DMA
    scratch = [
        pltpu.VMEM((FEATS, PTS), F32), pltpu.VMEM((FEATS, PTS), F32),
        pltpu.VMEM((2, 3, PTS), F32), pltpu.VMEM((2, 64, PTS), BF16), pltpu.VMEM((4, 16, 128), F32),
        pltpu.VMEM((4, 3, 256), F32), pltpu.VMEM((4, 64, 256), BF16), pltpu.VMEM((80, FEATS), BF16),
        pltpu.VMEM((128, 256), F32), pltpu.VMEM((FEATS, 128), BF16), pltpu.VMEM((64, PTS), F32),
        pltpu.VMEM((128, PTS), BF16), pltpu.VMEM((128, PTS), BF16),
        pltpu.VMEM((FEATS, 128), F32), pltpu.VMEM((FEATS, 128), F32),
        pltpu.VMEM((ROUNDS, 8, 128), F32), pltpu.VMEM((ROUNDS, PEERS, 8, 128), F32),
        pltpu.VMEM((ROUNDS, 2, 8, 128), F32), pltpu.VMEM((ROUNDS, 2, 8, 128), F32),
    ] + [pltpu.VMEM((STEPS + 2, 8, 128), F32)] * 4 + [pltpu.VMEM((STEPS + 1, 16, 128), F32)] * 6 + [
        pltpu.VMEM((16, FEATS), F32), pltpu.VMEM((16, PTS), F32),
        pltpu.VMEM((80, PTS), F32), pltpu.VMEM((80, PTS), F32),
        pltpu.VMEM((2, 64, HALF), F32), pltpu.VMEM((2, 64, HALF), F32), pltpu.VMEM((2, 64, HALF), F32),
        dma((8,)), dma((2, 3)), dma((2,)), dma((ROUNDS,)), dma((ROUNDS,)), dma((ROUNDS, 2)), dma((ROUNDS, 2)),
        dma((2,)), dma((2,)), dma((2,)), dma((2, 4)), dma((2, 4)), dma((2, 3)), dma((2, 3)),
    ]
    return pl.pallas_call(
        kernel,
        out_shape=(out, out),
        in_specs=[hbm] * 8 + [vmem] * 2,
        out_specs=(hbm, hbm),
        scratch_shapes=scratch,
        compiler_params=pltpu.CompilerParams(
            collective_id=0, has_side_effects=True, vmem_limit_bytes=56 * 2**20
        ),
    )(points_x, emb_x, points_y, emb_y, *vectors, omega_coord, omega_emb)


def solution(mesh):
    in_specs = (
        P(None, "pts"),
        P(None, "pts"),
        P(None, "pts"),
        P(None, "pts"),
        P("pts"),
        P("pts"),
        P("pts"),
        P("pts"),
        P(None, "feat"),
        P(None, "feat"),
    )
    out_specs = (P(None, "pts"), P(None, "pts"))
    return jax.shard_map(
        per_device, mesh=mesh, in_specs=in_specs, out_specs=out_specs, check_vma=False
    )
```

time: 1050 us -> 167 us (0.16); the launches traced: 1040 us -> 166 us
  blocking collectives: 704 us -> 0 us
  matrix products: 236 us -> 0 us
  Pallas kernels: 0 us -> 160 us
  waiting for transfers between devices: 68 us -> 0 us
  between operations: 14.5 us -> 0.65 us
    psum x23 -> x0, blocking collectives: 704 us -> none  [the longest x12 443 us: over_points(): return lax.psum(vector, 'pts')]
    dot_general x31 -> x0, matrix products: 236 us -> none  [the longest x3 26.7 us: transport_reverse_pass(): col_d = over_points(jnp.dot(feat_x, dual_u, precision=highest))]
    pallas_call x0 -> x1, Pallas kernels: none -> 160 us  [per_device(): pl.pallas_call(kernel, out_shape=(out, out), in_specs=[hbm] * 8 + [vmem]...]
    psum x1 -> x0, waiting for transfers between devices: 68 us -> none  [per_device(): grad_x, grad_y = lax.psum((share_x, share_y), 'feat')]
  transfers between devices with their start and end apart: 1 -> 0, of which waited for: 1 -> 0; matrix products, arithmetic and copies ran while one was open for 0% -> 0% of each run, Pallas kernels for 0% -> 0%
where the time goes in v1:
time: 167 us; the launch traced here: 166 us
  Pallas kernels  160 us (96%)
  local copies, waits for them, and re-layouts  4.53 us (3%)
    pallas_call x1, Pallas kernels, per_device(): pl.pallas_call(kernel, out_shape=(out, out), in_specs=[hbm] * 8 + [vmem]...  160 us
    unnamed x4, local copies, waits for them, and re-layouts  4.53 us

profile of v1, /device:TPU:0, one launch (start us, length us, event | category | flops | bytes accessed | tf_op | source)
XLA Modules:
  0.0 165.5 jit_solution(16525246267443053599)
XLA Ops:
  0.6 160.4 %shard_map.113 = (f32[64,8192]{1,0:T(8,128)}, f32[64,8192]{1,0:T(8,128)}) custom-call(f32[3,8192]{1,0:T(4,128)} %points_x.1, bf16[64,8192]{1,0:T(8,128)(2,1)} %emb_x.1, f32[3,8192]{1,0:T(4,128)} %points_y.1, bf16[64,8192]{1,0:T(8,128)(2,1)} %emb_y.1, f32[64,128]{1,0:T(8,128)} %bitcast.4, f32[64,128]{1,0:T(8,128)} %bitcast.5, f32[64,128]{1,0:T(8,128)} %bitcast.6, ...), custom_call_target="tpu_custom_call" | custom-call | tf_op jit(solution)/shard_map/pallas_call | solution.py:422
  161.0 0.0 copy-start
  161.0 3.2 %copy.14 = f32[64,8192]{1,0:T(8,128)} copy(f32[64,8192]{1,0:T(8,128)} %get-tuple-element.4) | data formatting | bytes 4194304
  164.2 0.0 copy-done
  164.2 1.3 copy.15
Async XLA Ops:
  161.0 3.2 %copy-start = (f32[64,8192]{1,0:T(8,128)S(1)}, f32[64,8192]{1,0:T(8,128)}, u32[]{:S(2)}) copy-start(f32[64,8192]{1,0:T(8,128)} %get-tuple-element.5) | copy-start | bytes 6291460
